TPU v7x, 32 devices: a whole 2x2x4 slice. The times are simulated.
32 devices in a mesh: dp: 4 (over z), mp: 8 (over y, x, core).
Axes of the slice: x: 2, y: 2, z: 4, core: 2. Of those that a mesh axis runs over, the one named last changes fastest.
Arguments:
- guess_vectors: bfloat16 [128, 16, 4096], P(('dp', 'mp')), may hold values from -6 to 6
- preceding_symbol_vector: bfloat16 [128, 4096], P(('dp', 'mp')), may hold values from -6 to 6
- earlier_memory_matrix: float32 [128, 64, 64, 64], P('dp', 'mp'), may hold values from -4 to 4
- lag_blend_factor: float32 [4096], replicated, may hold values from 0 to 1
- constant_lag_blends: float32 [5, 4096], replicated, may hold values from 0 to 1
- blending_lower_matrix: bfloat16 [4096, 160], replicated, may hold values from -0.09375 to 0.09375
- blending_raise_matrix: bfloat16 [5, 32, 4096], replicated, may hold values from -1 to 1
- constant_fading: float32 [4096], P('mp'), may hold values from -6 to -1
- fading_lower_matrix: bfloat16 [4096, 64], replicated, may hold values from -0.09375 to 0.09375
- fading_raise_matrix: bfloat16 [64, 4096], P(None, 'mp'), may hold values from -1 to 1
- diagonal_boost: float32 [64, 64], P('mp'), may hold values from -3 to 3
- acceptor_matrix: bfloat16 [4096, 4096], P('dp', 'mp'), may hold values from -0.09375 to 0.09375
- lookup_matrix: bfloat16 [4096, 4096], P('dp', 'mp'), may hold values from -0.09375 to 0.09375
- payload_matrix: bfloat16 [4096, 4096], P('dp', 'mp'), may hold values from -0.09375 to 0.09375
- gating_matrix: bfloat16 [4096, 4096], P('dp', 'mp'), may hold values from -0.09375 to 0.09375
- emission_matrix: bfloat16 [4096, 4096], P('mp', 'dp'), may hold values from -0.09375 to 0.09375
- groupwise_scaling_factor: float32 [4096], P('mp'), may hold values from 0.1 to 1.9
- groupwise_scaling_offset: float32 [4096], P('mp'), may hold values from -3 to 3
- usable_guess_amount: int32 [128], replicated, may hold values from 1 to 16, as said below
- approved_guesses: int32 [128], replicated, may hold values from 0 to 16, as said below
- destination_slot: int32 [128], replicated, may hold values from 0 to 127, as said below
Outputs:
- layer_out: bfloat16 [128, 16, 4096], P(('dp', 'mp'))
- next_state: float32 [128, 64, 64, 64], P('dp', 'mp')
- next_edge: bfloat16 [128, 4096], P('dp', 'mp')
Inputs may be any that keep to these rules, and one draw needn't show every extreme that they name: `usable_guess_amount`: some request has all 16 draft tokens valid. approved_guesses[b] <= usable_guess_amount[b]; some request accepts all 16. destination_slot is a permutation of the requests. Of the 32 requests of one aligned block, at most 16 have owner slots in one aligned block of 32 slots, and some pair of blocks reaches 16.
All inputs are finite; a program needn't handle non-finite values.
Results may differ from a plain program's by a relative error of at most 0.007.
Values may be sent and summed in bfloat16 or wider, within the bound.
A program may use at most 256 MiB of HBM per device.

v0:
```python
import jax
import jax.numpy as jnp
from jax import lax
from jax.sharding import PartitionSpec as P

GROUP_DIMENSION = 64
norm_eps = 0.00064


def token_mixes(
    guess_vectors,
    edges,
    lag_blend_factor,
    constant_lag_blends,
    blending_lower_matrix,
    blending_raise_matrix,
):
    previous = jnp.concatenate([edges[:, None, :], guess_vectors[:, :-1, :]], axis=1)
    width = guess_vectors.shape[-1]
    current_input = guess_vectors.reshape(-1, width).astype(jnp.float32)
    shift_difference = previous.reshape(-1, width).astype(jnp.float32) - current_input
    shift_blended = (current_input + shift_difference * lag_blend_factor).astype(jnp.bfloat16)
    mixing_inner_all = jnp.tanh(
        jnp.dot(shift_blended, blending_lower_matrix, preferred_element_type=jnp.float32)
    ).astype(jnp.bfloat16)
    mixing_inner_width = blending_raise_matrix.shape[1]
    shift_mixed_rows = []
    for mix_component in range(5):
        mixing_inner_part = jnp.dot(
            mixing_inner_all[
                :, mix_component * mixing_inner_width : (mix_component + 1) * mixing_inner_width
            ],
            blending_raise_matrix[mix_component],
            preferred_element_type=jnp.float32,
        )
        shift_mixed_rows.append(
            (
                current_input
                + shift_difference * (constant_lag_blends[mix_component] + mixing_inner_part)
            ).astype(jnp.bfloat16)
        )
    return shift_mixed_rows


def wkv_blocks(
    acceptor_vectors,
    lookup_vectors,
    payload_vectors,
    logarithmic_fading_entries,
    diagonal_boost,
    starting_memory,
    approved_guesses,
):
    draft = acceptor_vectors.shape[1]
    cumulative = jnp.cumsum(logarithmic_fading_entries, axis=1)
    starts = jnp.concatenate(
        [jnp.zeros_like(logarithmic_fading_entries[:, :1]), cumulative], axis=1
    )
    before = starts[:, :draft]
    from_start = jnp.einsum(
        "bthi,bhij->bthj",
        acceptor_vectors * jnp.exp(before),
        starting_memory,
        precision=lax.Precision.HIGHEST,
    )
    later = jnp.arange(draft)[:, None] > jnp.arange(draft)[None, :]
    exponent = before[:, :, None] - cumulative[:, None, :]
    exponent = jnp.where(later[None, :, :, None, None], exponent, -1e30)
    scores = jnp.sum(
        acceptor_vectors[:, :, None] * lookup_vectors[:, None, :] * jnp.exp(exponent), axis=-1
    )
    inner = jnp.einsum("btsh,bshj->bthj", scores, payload_vectors, precision=lax.Precision.HIGHEST)
    diagonal_boost_contribution = (
        jnp.sum(acceptor_vectors * diagonal_boost * lookup_vectors, axis=-1, keepdims=True)
        * payload_vectors
    )
    outputs = from_start + inner + diagonal_boost_contribution
    at_accept = jnp.take_along_axis(starts, approved_guesses[:, None, None, None], axis=1)[:, 0]
    used = jnp.arange(draft)[None, :] < approved_guesses[:, None]
    coef_exp = jnp.where(used[:, :, None, None], at_accept[:, None] - cumulative, -1e30)
    weighted = jnp.exp(coef_exp) * lookup_vectors
    picked = jnp.exp(at_accept)[..., None] * starting_memory + jnp.einsum(
        "bshi,bshj->bhij", weighted, payload_vectors, precision=lax.Precision.HIGHEST
    )
    return (outputs, picked)


def gated_norm(outputs, gate_raw, gain, bias):
    centre = jnp.mean(outputs, axis=-1, keepdims=True)
    spread = outputs - centre
    variance = jnp.mean(spread * spread, axis=-1, keepdims=True)
    normed = (spread * lax.rsqrt(variance + norm_eps)).reshape(outputs.shape[0], -1)
    return ((normed * gain + bias) * jax.nn.silu(gate_raw)).astype(jnp.bfloat16)


def on_device(
    guess_vectors,
    preceding_symbol_vector,
    earlier_memory_matrix,
    lag_blend_factor,
    constant_lag_blends,
    blending_lower_matrix,
    blending_raise_matrix,
    constant_fading,
    fading_lower_matrix,
    fading_raise_matrix,
    diagonal_boost,
    acceptor_matrix,
    lookup_matrix,
    payload_matrix,
    gating_matrix,
    emission_matrix,
    groupwise_scaling_factor,
    groupwise_scaling_offset,
    usable_guess_amount,
    approved_guesses,
    destination_slot,
):
    own_reqs, draft, width = guess_vectors.shape
    group_count = lax.axis_size("mp")
    row_groups = lax.axis_size("dp")
    row_reqs = own_reqs * group_count
    row_index = lax.axis_index("dp")
    group_index = lax.axis_index("mp")
    local_width = acceptor_matrix.shape[1]
    local_heads = local_width // GROUP_DIMENSION
    gathered, edges_all = (
        lax.all_gather(guess_vectors, "mp", axis=0, tiled=True),
        lax.all_gather(preceding_symbol_vector, "mp", axis=0, tiled=True),
    )
    shift_mixed_rows = token_mixes(
        gathered,
        edges_all,
        lag_blend_factor,
        constant_lag_blends,
        blending_lower_matrix,
        blending_raise_matrix,
    )
    token_rows = row_reqs * draft
    sources = (shift_mixed_rows[3], shift_mixed_rows[1], shift_mixed_rows[2], shift_mixed_rows[4])
    pieces = (
        lax.all_gather(acceptor_matrix, "dp", axis=0, tiled=True),
        lax.all_gather(lookup_matrix, "dp", axis=0, tiled=True),
        lax.all_gather(payload_matrix, "dp", axis=0, tiled=True),
        lax.all_gather(gating_matrix, "dp", axis=0, tiled=True),
    )
    acceptor_vectors, lookup_vectors, payload_vectors, gate_raw = tuple(
        (
            jnp.dot(source_rows, piece, preferred_element_type=jnp.float32)
            for source_rows, piece in zip(sources, pieces)
        )
    )
    decay_inner_rows = jnp.tanh(
        jnp.dot(shift_mixed_rows[0], fading_lower_matrix, preferred_element_type=jnp.float32)
    ).astype(jnp.bfloat16)
    logarithmic_fading_entries = -jnp.exp(
        constant_fading
        + jnp.dot(decay_inner_rows, fading_raise_matrix, preferred_element_type=jnp.float32)
    )

    def to_heads(values):
        return values.reshape(row_reqs, draft, local_heads, GROUP_DIMENSION)

    row_accepted = lax.dynamic_slice_in_dim(approved_guesses, row_index * row_reqs, row_reqs)
    outputs, picked = wkv_blocks(
        to_heads(acceptor_vectors),
        to_heads(lookup_vectors),
        to_heads(payload_vectors),
        to_heads(logarithmic_fading_entries),
        diagonal_boost,
        earlier_memory_matrix,
        row_accepted,
    )
    hidden = gated_norm(
        outputs.reshape(token_rows, local_heads, GROUP_DIMENSION),
        gate_raw,
        groupwise_scaling_factor,
        groupwise_scaling_offset,
    )
    out_cols = lax.all_gather(emission_matrix, "dp", axis=1, tiled=True)
    attended = lax.psum_scatter(
        jnp.dot(hidden, out_cols, preferred_element_type=jnp.float32).astype(jnp.bfloat16),
        "mp",
        scatter_dimension=0,
        tiled=True,
    ).astype(jnp.float32)
    own_start = (row_index * group_count + group_index) * own_reqs
    own_lengths = lax.dynamic_slice_in_dim(usable_guess_amount, own_start, own_reqs)
    valid_mask = jnp.arange(draft, dtype=jnp.int32)[None, :] < own_lengths[:, None]
    layer_out = (
        guess_vectors.astype(jnp.float32)
        + jnp.where(
            valid_mask[..., None],
            attended.reshape(own_reqs, draft, width),
            jnp.zeros((), jnp.float32),
        )
    ).astype(jnp.bfloat16)
    edge_rows = jnp.concatenate([edges_all[:, None, :], gathered], axis=1)
    edge_cols = lax.dynamic_slice_in_dim(edge_rows, group_index * local_width, local_width, 2)
    chosen = jnp.take_along_axis(edge_cols, row_accepted[:, None, None], axis=1)[:, 0]
    capacity = 2 * row_reqs // row_groups
    target_rows = (destination_slot // row_reqs).reshape(row_groups, row_reqs)
    onehot = (
        target_rows[:, :, None] == jnp.arange(row_groups, dtype=jnp.int32)[None, None, :]
    ).astype(jnp.int32)
    earlier = jnp.cumsum(onehot, axis=1) - onehot
    ranks = jnp.sum(earlier * onehot, axis=-1)
    my_targets = lax.dynamic_index_in_dim(target_rows, row_index, 0, keepdims=False)
    my_ranks = lax.dynamic_index_in_dim(ranks, row_index, 0, keepdims=False)
    selected = (
        my_targets[:, None, None] == jnp.arange(row_groups, dtype=jnp.int32)[None, :, None]
    ) & (my_ranks[:, None, None] == jnp.arange(capacity, dtype=jnp.int32)[None, None, :])
    source_index = jnp.sum(
        selected.astype(jnp.int32) * jnp.arange(row_reqs, dtype=jnp.int32)[:, None, None], axis=0
    )
    filled = jnp.any(selected, axis=0)
    send_state = jnp.where(
        filled[..., None, None, None], picked[source_index], jnp.zeros((), jnp.float32)
    )
    send_edge = jnp.where(
        filled[..., None], chosen[source_index].astype(jnp.float32), jnp.zeros((), jnp.float32)
    )
    recv_state, recv_edge = (
        lax.all_to_all(
            send_state.astype(jnp.bfloat16), "dp", split_axis=0, concat_axis=0, tiled=True
        ).astype(send_state.dtype),
        lax.all_to_all(
            send_edge.astype(jnp.bfloat16), "dp", split_axis=0, concat_axis=0, tiled=True
        ).astype(send_edge.dtype),
    )
    wanted = row_index * row_reqs + jnp.arange(row_reqs, dtype=jnp.int32)
    total_reqs = destination_slot.shape[0]
    matches = (destination_slot[None, :] == wanted[:, None]).astype(jnp.int32)
    which = jnp.sum(matches * jnp.arange(total_reqs, dtype=jnp.int32)[None, :], axis=1)
    flat_index = which // row_reqs * capacity + ranks.reshape(-1)[which]
    next_state = recv_state.reshape(
        row_groups * capacity, local_heads, GROUP_DIMENSION, GROUP_DIMENSION
    )[flat_index]
    next_edge = recv_edge.reshape(row_groups * capacity, local_width)[flat_index].astype(
        jnp.bfloat16
    )
    return (layer_out, next_state, next_edge)


def solution(mesh):
    in_specs = (
        P(("dp", "mp"), None, None),
        P(("dp", "mp"), None),
        P("dp", "mp", None, None),
        P(),
        P(),
        P(),
        P(),
        P("mp"),
        P(),
        P(None, "mp"),
        P("mp", None),
        P("dp", "mp"),
        P("dp", "mp"),
        P("dp", "mp"),
        P("dp", "mp"),
        P("mp", "dp"),
        P("mp"),
        P("mp"),
        P(),
        P(),
        P(),
    )
    out_specs = (P(("dp", "mp"), None, None), P("dp", "mp", None, None), P("dp", "mp"))
    return jax.shard_map(
        on_device, mesh=mesh, in_specs=in_specs, out_specs=out_specs, check_vma=False
    )
```

profile of v0, /device:TPU:0, one launch (start us, length us, event | category | flops | bytes accessed | tf_op | source)
XLA Modules:
  0.0 585.9 jit_solution(18396825524794450216)
XLA Ops:
  12.2 10.8 %all-gather = bf16[8,4,4096]{2,1,0:T(4,128)(2,1)S(1)} all-gather(bf16[1,4,4096]{2,1,0:T(4,128)(2,1)S(1)} %bitcast.122), channel_id=1, replica_groups=mesh['dp'=4,'mp'=8] {'mp'}, dimensions={0}, use_global_device_ids=true | all-gather | bytes 294912 | tf_op jit(solution)/shard_map/all_gather | solution.py:129
  23.9 25.6 %all-gather.8.cloned.1.call-done = bf16[32,16,4096]{2,1,0:T(8,128)(2,1)} async-done(((bf16[4,16,4096]{2,1,0:T(8,128)(2,1)}), bf16[32,16,4096]{2,1,0:T(8,128)(2,1)}) %all-gather.8.cloned.1.call-update) | async-done | bytes 4194320 | tf_op jit(solution)/shard_map/all_gather | solution.py:128
  57.1 74.7 %all-gather.12.cloned.1.call-done = bf16[4096,512]{1,0:T(8,128)(2,1)} async-done(((bf16[1024,512]{1,0:T(8,128)(2,1)}), bf16[4096,512]{1,0:T(8,128)(2,1)}) %all-gather.12.cloned.1.call-update) | async-done | bytes 4194320 | tf_op jit(solution)/shard_map/all_gather | solution.py:144
  131.8 8.5 %fusion.23 = f32[512,512]{1,0:T(8,128)S(1)} fusion(bf16[4096,512]{1,0:T(8,128)(2,1)} %all-gather.12.cloned.1.call-done, bf16[512,4096]{1,0:T(8,128)(2,1)} %bitcast.105, bf16[512,4096]{1,0:T(8,128)(2,1)} %bitcast.112, f32[4096]{0:T(1024)S(1)} %bitcast.127, bf16[5,32,4096]{2,1,0:T(8,128)(2,1)} %param.27, bf16[512,160]{0,1:T(8,128)(2,1)S(1)} %fusion.28), kind=kOutput, calls=%fused_computation.48 | convolution fusion | flops 2296381440 | bytes 13942784 | tf_op jit(solution)/shard_map/dot_general | solution.py:149
  142.2 70.5 %all-gather.14.cloned.1.call-done = bf16[4096,512]{1,0:T(8,128)(2,1)} async-done(((bf16[1024,512]{1,0:T(8,128)(2,1)}), bf16[4096,512]{1,0:T(8,128)(2,1)}) %all-gather.14.cloned.1.call-update) | async-done | bytes 4194320 | tf_op jit(solution)/shard_map/all_gather | solution.py:143
  212.7 8.6 %fusion.22 = f32[512,512]{1,0:T(8,128)S(1)} fusion(bf16[4096,512]{1,0:T(8,128)(2,1)} %all-gather.14.cloned.1.call-done, bf16[512,4096]{1,0:T(8,128)(2,1)} %bitcast.106, bf16[512,4096]{1,0:T(8,128)(2,1)} %bitcast.113, f32[4096]{0:T(1024)S(1)} %bitcast.126, bf16[5,32,4096]{2,1,0:T(8,128)(2,1)} %param.27, bf16[512,160]{0,1:T(8,128)(2,1)S(1)} %fusion.28), kind=kOutput, calls=%fused_computation.47 | convolution fusion | flops 2296381440 | bytes 13942784 | tf_op jit(solution)/shard_map/dot_general | solution.py:149
  223.1 6.9 %fusion.32 = bf16[512,64]{0,1:T(8,128)(2,1)S(1)} fusion(bf16[4096,64]{0,1:T(8,128)(2,1)S(1)} %copy-done.19, bf16[512,4096]{1,0:T(8,128)(2,1)} %bitcast.107, bf16[512,4096]{1,0:T(8,128)(2,1)} %bitcast.114, f32[4096]{0:T(1024)S(1)} %bitcast.125, bf16[5,32,4096]{2,1,0:T(8,128)(2,1)} %param.27, bf16[512,160]{0,1:T(8,128)(2,1)S(1)} %fusion.28), kind=kOutput, calls=%fused_computation.53 | convolution fusion | flops 417366016 | bytes 9289728 | tf_op jit(solution)/shard_map/dot_general | solution.py:154
  234.1 59.4 %all-gather.10.cloned.1.call-done = bf16[4096,512]{1,0:T(8,128)(2,1)} async-done(((bf16[1024,512]{1,0:T(8,128)(2,1)}), bf16[4096,512]{1,0:T(8,128)(2,1)}) %all-gather.10.cloned.1.call-update) | async-done | bytes 4194320 | tf_op jit(solution)/shard_map/all_gather | solution.py:142
  293.4 8.6 %fusion.24 = f32[512,512]{1,0:T(8,128)S(1)} fusion(bf16[4096,512]{1,0:T(8,128)(2,1)} %all-gather.10.cloned.1.call-done, bf16[512,4096]{1,0:T(8,128)(2,1)} %bitcast.108, bf16[512,4096]{1,0:T(8,128)(2,1)} %bitcast.115, f32[4096]{0:T(1024)S(1)} %bitcast.124, bf16[5,32,4096]{2,1,0:T(8,128)(2,1)} %param.27, bf16[512,160]{0,1:T(8,128)(2,1)} %copy-done.25), kind=kOutput, calls=%fused_computation.49 | convolution fusion | flops 2296381440 | bytes 13942784 | tf_op jit(solution)/shard_map/dot_general | solution.py:149
  307.7 6.3 %exponential_multiply_fusion = (f32[32,16,8,64]{3,2,1,0:T(8,128)}, f32[32,16,8,64]{3,2,1,0:T(8,128)}, f32[32,16,8]{2,1,0:T(8,128)S(1)}, f32[32,16,8,64]{3,2,1,0:T(8,128)}) fusion(f32[32,16,8,64]{3,2,1,0:T(8,128)} %mul.159, f32[32,16,8,64]{3,2,1,0:T(8,128)S(1)} %fusion.77, f32[32,8,64]{2,1,0:T(8,128)S(1)} %get-tuple-element.4, ...), kind=kLoop, calls=%fused_computation.35 | loop fusion | flops 1830912 | bytes 6375936 | tf_op jit(solution)/shard_map/mul | solution.py:81
  314.0 15.2 %multiply_reduce_fusion = f32[32,16,16,8]{3,2,1,0:T(8,128)} fusion(f32[32,16,8,64]{3,2,1,0:T(8,128)S(1)} %fusion.77, f32[32,16,8,64]{3,2,1,0:T(8,128)} %get-tuple-element.10, f32[32,16,8,64]{3,2,1,0:T(8,128)} %mul.159, f32[32,16,8,64]{3,2,1,0:T(8,128)} %reshape.354, pred[16,16]{1,0:T(8,128)(4,1)S(1)} %iota_compare_fusion.3), kind=kLoop, calls=%fused_computation.7 | loop fusion | flops 20905984 | bytes 4456704 | tf_op jit(solution)/shard_map/reduce_sum | solution.py:69
  333.3 10.2 %fusion.11 = f32[32,8,16,64]{3,2,1,0:T(8,128)S(1)} fusion(f32[32,8,64,64]{3,2,1,0:T(8,128)} %param.23, f32[32,16,8,64]{3,2,1,0:T(8,128)S(1)} %copy-done.6), kind=kOutput, calls=%fused_computation.33 | convolution fusion | flops 201326592 | bytes 6291456 | tf_op jit(solution)/shard_map/bthi,bhij->bthj/dot_general | solution.py:60
  354.2 19.7 %multiply_add_fusion = bf16[32,8,64,64]{3,2,1,0:T(8,128)(2,1)} fusion(f32[32,8,64,64]{3,2,1,0:T(8,128)} %param.23, f32[32,8,64]{2,1,0:T(8,128)S(1)} %get-tuple-element.3, f32[32,16,8,64]{3,2,1,0:T(8,128)} %get-tuple-element.7, f32[32,16,8,64]{3,2,1,0:T(8,128)} %reshape.356), kind=kOutput, calls=%fused_computation.23 | convolution fusion | flops 204472320 | bytes 8454144 | tf_op jit(solution)/shard_map/bshi,bshj->bhij/dot_general | solution.py:82
  373.9 7.8 %gather_fusion = bf16[64,8,64,64]{3,2,1,0:T(8,128)(2,1)} fusion(bf16[32,8,64,64]{3,2,1,0:T(8,128)(2,1)} %multiply_add_fusion, s32[1024]{0:T(1024)S(1)} %pad_clamp_fusion.2), kind=kCustom, calls=%fused_computation | custom fusion | bytes 8388864 | tf_op jit(solution)/shard_map/gather | solution.py:218
  386.7 10.5 %select_convert_fusion = bf16[4,16,8,64,64]{4,3,2,1,0:T(8,128)(2,1)} fusion(bf16[4,16,8,64,64]{4,3,2,1,0:T(8,128)(2,1)} %bitcast.103, pred[4,16]{1,0:T(4,128)(4,1)S(1)} %and_reduce_fusion), kind=kLoop, calls=%fused_computation.15 | loop fusion | flops 2097152 | bytes 8388672 | tf_op jit(solution)/shard_map/convert_element_type | solution.py:225
  403.4 9.7 %reshape.439 = bf16[4,2,262144]{2,1,0:T(2,128)(2,1)} reshape(bf16[4,16,8,64,64]{4,3,2,1,0:T(8,128)(2,1)} %select_convert_fusion) | data formatting | bytes 8388608
  413.1 5.1 all-to-all-start
  418.5 9.7 %multiply_convert_fusion = bf16[512,512]{1,0:T(8,128)(2,1)} fusion(bf16[4096,512]{1,0:T(8,128)(2,1)} %all-gather.16.cloned.1.call-done, bf16[512,4096]{1,0:T(8,128)(2,1)} %bitcast.109, bf16[512,4096]{1,0:T(8,128)(2,1)} %bitcast.116, f32[4096]{0:T(1024)S(1)} %bitcast.123, f32[512,512]{1,0:T(8,128)S(1)} %copy-done.12, f32[512,512]{1,0:T(8,128)S(1)} %copy-done.11, ...), kind=kOutput, calls=%fused_computation.57 | convolution fusion | flops 2299002880 | bytes 16568320 | tf_op jit(solution)/shard_map/dot_general | solution.py:149
  428.2 67.7 %all-gather.18.cloned.1.call-done = bf16[512,4096]{1,0:T(8,128)(2,1)} async-done(((bf16[512,1024]{1,0:T(8,128)(2,1)}), bf16[512,4096]{1,0:T(8,128)(2,1)}) %all-gather.18.cloned.1.call-update) | async-done | bytes 4194320 | tf_op jit(solution)/shard_map/all_gather | solution.py:180
  495.9 6.7 %convolution_convert_fusion = bf16[512,4096]{1,0:T(8,128)(2,1)} fusion(bf16[512,512]{1,0:T(8,128)(2,1)} %multiply_convert_fusion, bf16[512,4096]{1,0:T(8,128)(2,1)} %all-gather.18.cloned.1.call-done), kind=kOutput, calls=%fused_computation.24 | convolution fusion | flops 2149580800 | bytes 8912896 | tf_op jit(solution)/shard_map/dot_general | solution.py:182
  505.6 40.1 %all-to-all-done = bf16[4,2,262144]{2,1,0:T(2,128)(2,1)} async-done(((bf16[4,2,262144]{2,1,0:T(2,128)(2,1)}), bf16[4,2,262144]{2,1,0:T(2,128)(2,1)}, u32[]{:S(2)}, u32[]{:S(2)}) %all-to-all-start) | async-done | bytes 4194336 | tf_op jit(solution)/shard_map/all_to_all | solution.py:224
  545.7 9.3 %reshape.440 = bf16[4,16,8,64,64]{4,3,2,1,0:T(8,128)(2,1)} reshape(bf16[4,2,262144]{2,1,0:T(2,128)(2,1)} %all-to-all-done) | data formatting | bytes 8388608
  555.0 11.3 %bitcast_convert_fusion = f32[64,8,64,64]{3,2,1,0:T(8,128)} fusion(bf16[4,16,8,64,64]{4,3,2,1,0:T(8,128)(2,1)} %reshape.440), kind=kLoop, calls=%fused_computation.22 | loop fusion | flops 2097152 | bytes 12582912 | tf_op jit(solution)/shard_map/reshape | solution.py:236
  566.3 10.4 %gather_fusion.2 = f32[32,8,64,64]{3,2,1,0:T(8,128)} fusion(f32[64,8,64,64]{3,2,1,0:T(8,128)} %bitcast_convert_fusion, s32[1024]{0:T(1024)S(1)} %pad_clamp_fusion), kind=kCustom, calls=%fused_computation.2 | custom fusion | bytes 8388736 | tf_op jit(solution)/shard_map/gather | solution.py:236
  (141 shorter events, 57.6 us)
Async XLA Ops:
  7.2 47.9 %copy-start = (bf16[4096,160]{0,1:T(8,128)(2,1)S(1)}, bf16[4096,160]{0,1:T(8,128)(2,1)}, u32[]{:S(2)}) copy-start(bf16[4096,160]{0,1:T(8,128)(2,1)} %param.26) | copy-start | bytes 3932164
  7.2 16.4 %copy-start.14 = (f32[5,4096]{1,0:T(8,128)S(1)}, f32[5,4096]{1,0:T(8,128)}, u32[]{:S(2)}) copy-start(f32[5,4096]{1,0:T(8,128)} %param.25) | copy-start | bytes 245764
  7.2 42.2 %all-gather.8.cloned.1.call-start = ((), (), s32[]{:S(2)}) async-start(), calls=%async_computation.3 | async-start | bytes 4718592 | tf_op jit(solution)/shard_map/all_gather | solution.py:128
  8.0 123.8 %all-gather.12.cloned.1.call-start = ((), (), s32[]{:S(2)}) async-start(), calls=%async_computation.5 | async-start | bytes 5242880 | tf_op jit(solution)/shard_map/all_gather | solution.py:144
  8.7 204.0 %all-gather.14.cloned.1.call-start = ((), (), s32[]{:S(2)}) async-start(), calls=%async_computation.6 | async-start | bytes 5242880 | tf_op jit(solution)/shard_map/all_gather | solution.py:143
  9.4 284.0 %all-gather.10.cloned.1.call-start = ((), (), s32[]{:S(2)}) async-start(), calls=%async_computation.4 | async-start | bytes 5242880 | tf_op jit(solution)/shard_map/all_gather | solution.py:142
  10.0 408.5 %all-gather.16.cloned.1.call-start = ((), (), s32[]{:S(2)}) async-start(), calls=%async_computation.7 | async-start | bytes 5242880 | tf_op jit(solution)/shard_map/all_gather | solution.py:145
  10.6 485.3 %all-gather.18.cloned.1.call-start = ((), (), s32[]{:S(2)}) async-start(), calls=%async_computation.8 | async-start | bytes 5242880 | tf_op jit(solution)/shard_map/all_gather | solution.py:180
  23.1 30.1 %copy-start.8 = (bf16[32,1,4096]{2,0,1:T(8,128)(2,1)}, bf16[32,1,4096]{2,0,1:T(8,128)(2,1)S(1)}, u32[]{:S(2)}) copy-start(bf16[32,1,4096]{2,0,1:T(8,128)(2,1)S(1)} %broadcast_in_dim.75) | copy-start | bytes 786436
  49.4 5.7 copy-start.3
  49.4 5.7 copy-start.20
  57.1 166.0 %copy-start.25 = (bf16[512,160]{0,1:T(8,128)(2,1)}, bf16[512,160]{0,1:T(8,128)(2,1)S(1)}, u32[]{:S(2)}) copy-start(bf16[512,160]{0,1:T(8,128)(2,1)S(1)} %fusion.28) | copy-start | bytes 491524
  212.7 10.4 %copy-start.19 = (bf16[4096,64]{0,1:T(8,128)(2,1)S(1)}, bf16[4096,64]{0,1:T(8,128)(2,1)}, u32[]{:S(2)}) copy-start(bf16[4096,64]{0,1:T(8,128)(2,1)} %param.29) | copy-start | bytes 1572868
  223.1 6.9 %copy-start.13 = (bf16[64,512]{1,0:T(8,128)(2,1)S(1)}, bf16[64,512]{1,0:T(8,128)(2,1)}, u32[]{:S(2)}) copy-start(bf16[64,512]{1,0:T(8,128)(2,1)} %param.30) | copy-start | bytes 196612
  223.1 6.9 %copy-start.17 = (f32[512]{0:T(512)S(1)}, f32[512]{0:T(512)}, u32[]{:S(2)}) copy-start(f32[512]{0:T(512)} %param.28) | copy-start | bytes 6148
  302.0 5.6 copy-start.16
  333.3 10.2 %copy-start.2 = (f32[32,16,8,64]{3,2,1,0:T(8,128)S(1)}, f32[32,16,8,64]{3,2,1,0:T(8,128)}, u32[]{:S(2)}) copy-start(f32[32,16,8,64]{3,2,1,0:T(8,128)} %reshape.356) | copy-start | bytes 3145732
  333.3 10.2 %copy-start.5 = (f32[32,16,16,8]{2,1,3,0:T(8,128)S(1)}, f32[32,16,16,8]{2,1,3,0:T(8,128)}, u32[]{:S(2)}) copy-start(f32[32,16,16,8]{2,1,3,0:T(8,128)} %copy.69) | copy-start | bytes 786436
  383.2 29.9 %all-to-all-start.1 = ((bf16[4,16,512]{2,1,0:T(8,128)(2,1)}), bf16[4,16,512]{2,1,0:T(8,128)(2,1)S(1)}, u32[]{:S(2)}, u32[]{:S(2)}) async-start(bf16[4,16,512]{2,1,0:T(8,128)(2,1)} %fusion.56), calls=%async_computation.2 | async-start | bytes 131072 | tf_op jit(solution)/shard_map/all_to_all | solution.py:227
  413.1 5.5 copy-start.22
  413.1 132.6 %all-to-all-start = ((bf16[4,2,262144]{2,1,0:T(2,128)(2,1)}), bf16[4,2,262144]{2,1,0:T(2,128)(2,1)}, u32[]{:S(2)}, u32[]{:S(2)}) async-start(bf16[4,2,262144]{2,1,0:T(2,128)(2,1)} %reshape.439), calls=%async_computation.1 | async-start | bytes 8388608 | tf_op jit(solution)/shard_map/all_to_all | solution.py:224
  418.2 158.5 %reduce-scatter.2.cloned.1.call-start = ((), (), s32[]{:S(2)}) async-start(), calls=%async_computation.9 | async-start | bytes 4718592 | tf_op jit(solution)/shard_map/reduce_scatter | solution.py:181
  566.3 10.4 %copy-start.10 = (bf16[4,16,4096]{2,1,0:T(8,128)(2,1)S(1)}, bf16[4,16,4096]{2,1,0:T(8,128)(2,1)}, u32[]{:S(2)}) copy-start(bf16[4,16,4096]{2,1,0:T(8,128)(2,1)} %param.21) | copy-start | bytes 1572868
  566.3 12.5 %copy-start.1 = (bf16[4096,160]{0,1:T(8,128)(2,1)S(1)}, bf16[4096,160]{0,1:T(8,128)(2,1)}, u32[]{:S(2)}) copy-start(bf16[4096,160]{0,1:T(8,128)(2,1)} %param.26) | copy-start | bytes 3932164
  (11 other events, 42.5 us)
Sparse Core Ops, SparseCore 0:
  9.9 39.4 all-gather.7
  51.0 80.7 all-gather.11
  133.4 79.2 all-gather.13
  214.1 79.2 all-gather.9
  294.9 79.2 all-gather.15
  375.6 120.2 all-gather.17
  502.8 49.4 reduce-scatter.1
where the time goes:
time: 590 us; the launch traced here: 586 us
  waiting for transfers between devices  342 us (58%)
  matrix products  84.8 us (14%)
  local copies, waits for them, and re-layouts  70.2 us (12%)
  other arithmetic  54.3 us (9%)
  between operations  15 us (3%)
  blocking collectives  10.8 us (2%)
  starting transfers between devices  9.1 us (2%)
    all_gather x1, waiting for transfers between devices, on_device(): lax.all_gather(payload_matrix, 'dp', axis=0, tiled=True)  74.7 us
    all_gather x1, waiting for transfers between devices, on_device(): lax.all_gather(lookup_matrix, 'dp', axis=0, tiled=True)  70.5 us
    all_gather x1, waiting for transfers between devices, on_device(): out_cols = lax.all_gather(emission_matrix, 'dp', axis=1, tiled=True)  67.7 us
    all_gather x1, waiting for transfers between devices, on_device(): lax.all_gather(acceptor_matrix, 'dp', axis=0, tiled=True)  59.4 us
    all_to_all x1, waiting for transfers between devices, on_device(): lax.all_to_all(send_state.astype(jnp.bfloat16), 'dp', split_axis=0, conca...  40.1 us
    dot_general x4, matrix products, on_device(): jnp.dot(source_rows, piece, preferred_element_type=jnp.float32)  35.4 us
    all_gather x1, waiting for transfers between devices, on_device(): lax.all_gather(guess_vectors, 'mp', axis=0, tiled=True)  25.6 us
    unnamed x55, local copies, waits for them, and re-layouts  21.5 us
  transfers between devices with their start and end apart: 9, of which 6 were waited for; matrix products, arithmetic and copies ran while one was open for 35% of the time, Pallas kernels for 0%

commit v1 on v0

--- a/solution.py
+++ b/solution.py
@@ -5,6 +5,16 @@
 
 GROUP_DIMENSION = 64
 norm_eps = 0.00064
+
+
+def around_the_ring(x, name, along):
+    peers = lax.axis_size(name)
+    current, blocks = (x, [x])
+    for _ in range(peers - 1):
+        current = lax.ppermute(current, name, [(i, (i + 1) % peers) for i in range(peers)])
+        blocks.insert(0, current)
+    merged = jnp.concatenate(blocks, axis=along)
+    return jnp.roll(merged, (lax.axis_index(name) + 1) * x.shape[along], axis=along)
 
 
 def token_mixes(
@@ -177,7 +187,7 @@
         groupwise_scaling_factor,
         groupwise_scaling_offset,
     )
-    out_cols = lax.all_gather(emission_matrix, "dp", axis=1, tiled=True)
+    out_cols = around_the_ring(emission_matrix, "dp", 1)
     attended = lax.psum_scatter(
         jnp.dot(hidden, out_cols, preferred_element_type=jnp.float32).astype(jnp.bfloat16),
         "mp",

time: 590 us -> 550 us (0.932)
  waiting for transfers between devices: 342 us -> 285 us
  local copies, waits for them, and re-layouts: 70.2 us -> 86.5 us
    ppermute x0 -> x3, waiting for transfers between devices: none -> 85.4 us  [around_the_ring(): lax.ppermute(current, name, [(i, (i + 1) % peers) for i in range(peers)])]
    all_gather x1 -> x0, waiting for transfers between devices: 67.7 us -> none  [on_device(): out_cols = lax.all_gather(emission_matrix, 'dp', axis=1, tiled=True)]
    all_gather x1, waiting for transfers between devices: 59.4 us -> 9.76 us  [on_device(): lax.all_gather(acceptor_matrix, 'dp', axis=0, tiled=True)]
    all_to_all x1, waiting for transfers between devices: 40.1 us -> 73.8 us  [on_device(): lax.all_to_all(send_state.astype(jnp.bfloat16), 'dp', split_axis=0, conca...]
    all_gather x1, waiting for transfers between devices: 74.7 us -> 43 us  [on_device(): lax.all_gather(payload_matrix, 'dp', axis=0, tiled=True)]
    all_gather x1, waiting for transfers between devices: 25.6 us -> 0.01 us  [on_device(): lax.all_gather(guess_vectors, 'mp', axis=0, tiled=True)]
    unnamed x55 -> x58, local copies, waits for them, and re-layouts: 21.5 us -> 32.2 us
  transfers between devices with their start and end apart: 9 -> 11, of which waited for: 6 -> 7; matrix products, arithmetic and copies ran while one was open for 35% -> 40% of each run, Pallas kernels for 0% -> 0%
where the time goes in v1:
time: 550 us; the launch traced here: 546 us
  waiting for transfers between devices  285 us (52%)
  local copies, waits for them, and re-layouts  86.5 us (16%)
  matrix products  84.9 us (15%)
  other arithmetic  52.1 us (9%)
  between operations  15 us (3%)
  starting transfers between devices  12.2 us (2%)
  blocking collectives  10.5 us (2%)
    ppermute x3, waiting for transfers between devices, around_the_ring(): lax.ppermute(current, name, [(i, (i + 1) % peers) for i in range(peers)])  85.4 us
    all_to_all x1, waiting for transfers between devices, on_device(): lax.all_to_all(send_state.astype(jnp.bfloat16), 'dp', split_axis=0, conca...  73.8 us
    all_gather x1, waiting for transfers between devices, on_device(): lax.all_gather(lookup_matrix, 'dp', axis=0, tiled=True)  70.1 us
    all_gather x1, waiting for transfers between devices, on_device(): lax.all_gather(payload_matrix, 'dp', axis=0, tiled=True)  43 us
    dot_general x4, matrix products, on_device(): jnp.dot(source_rows, piece, preferred_element_type=jnp.float32)  35.5 us
    unnamed x58, local copies, waits for them, and re-layouts  32.2 us
    dot_general x1, matrix products, wkv_blocks(): jnp.einsum('bshi,bshj->bhij', weighted, payload_vectors, precision=lax.Pr...  19.7 us
    reduce_sum x1, other arithmetic, wkv_blocks(): jnp.sum(acceptor_vectors[:, :, None] * lookup_vectors[:, None, :] * jnp.e...  13.1 us
  transfers between devices with their start and end apart: 11, of which 7 were waited for; matrix products, arithmetic and copies ran while one was open for 40% of the time, Pallas kernels for 0%

profile of v1, /device:TPU:0, one launch (start us, length us, event | category | flops | bytes accessed | tf_op | source)
XLA Modules:
  0.0 545.9 jit_solution(14952629670545273738)
XLA Ops:
  13.9 24.6 %collective-permute-done = bf16[512,1024]{1,0:T(8,128)(2,1)S(1)} collective-permute-done((bf16[512,1024]{1,0:T(8,128)(2,1)}, bf16[512,1024]{1,0:T(8,128)(2,1)S(1)}, u32[]{:S(2)}, u32[]{:S(2)}) %collective-permute-start) | collective-permute-done | bytes 1048608 | tf_op jit(solution)/shard_map/ppermute | solution.py:14
  38.8 27.7 %collective-permute-done.1 = bf16[512,1024]{1,0:T(8,128)(2,1)} collective-permute-done((bf16[512,1024]{1,0:T(8,128)(2,1)S(1)}, bf16[512,1024]{1,0:T(8,128)(2,1)}, u32[]{:S(2)}, u32[]{:S(2)}) %collective-permute-start.1) | collective-permute-done | bytes 1048608 | tf_op jit(solution)/shard_map/ppermute | solution.py:14
  66.5 10.5 %all-gather = bf16[8,4,4096]{2,1,0:T(4,128)(2,1)} all-gather(bf16[1,4,4096]{2,1,0:T(4,128)(2,1)} %bitcast.121), channel_id=1, replica_groups=mesh['dp'=4,'mp'=8] {'mp'}, dimensions={0}, use_global_device_ids=true | all-gather | bytes 294912 | tf_op jit(solution)/shard_map/all_gather | solution.py:139
  82.5 33.1 %collective-permute-done.2 = bf16[512,1024]{1,0:T(8,128)(2,1)} collective-permute-done((bf16[512,1024]{1,0:T(8,128)(2,1)}, bf16[512,1024]{1,0:T(8,128)(2,1)}, u32[]{:S(2)}, u32[]{:S(2)}) %collective-permute-start.2) | collective-permute-done | bytes 1048608 | tf_op jit(solution)/shard_map/ppermute | solution.py:14
  134.7 7.0 %fusion.33 = bf16[512,64]{0,1:T(8,128)(2,1)S(1)} fusion(bf16[4096,64]{0,1:T(8,128)(2,1)S(1)} %copy-done.17, bf16[512,4096]{1,0:T(8,128)(2,1)} %bitcast.104, bf16[512,4096]{1,0:T(8,128)(2,1)} %bitcast.111, f32[4096]{0:T(1024)S(1)} %bitcast.126, bf16[5,32,4096]{2,1,0:T(8,128)(2,1)} %param.27, bf16[512,160]{0,1:T(8,128)(2,1)S(1)} %fusion.29), kind=kOutput, calls=%fused_computation.54 | convolution fusion | flops 417366016 | bytes 9289728 | tf_op jit(solution)/shard_map/dot_general | solution.py:164
  145.5 9.8 %all-gather.9.cloned.1.call-done = bf16[4096,512]{1,0:T(8,128)(2,1)} async-done(((bf16[1024,512]{1,0:T(8,128)(2,1)}), bf16[4096,512]{1,0:T(8,128)(2,1)}) %all-gather.9.cloned.1.call-update) | async-done | bytes 4194320 | tf_op jit(solution)/shard_map/all_gather | solution.py:152
  155.2 8.6 %fusion.25 = f32[512,512]{1,0:T(8,128)S(1)} fusion(bf16[4096,512]{1,0:T(8,128)(2,1)} %all-gather.9.cloned.1.call-done, bf16[512,4096]{1,0:T(8,128)(2,1)} %bitcast.105, bf16[512,4096]{1,0:T(8,128)(2,1)} %bitcast.112, f32[4096]{0:T(1024)S(1)} %bitcast.125, bf16[5,32,4096]{2,1,0:T(8,128)(2,1)} %param.27, bf16[512,160]{0,1:T(8,128)(2,1)} %copy-done.23), kind=kOutput, calls=%fused_computation.50 | convolution fusion | flops 2296381440 | bytes 13942784 | tf_op jit(solution)/shard_map/dot_general | solution.py:159
  165.5 70.1 %all-gather.13.cloned.1.call-done = bf16[4096,512]{1,0:T(8,128)(2,1)} async-done(((bf16[1024,512]{1,0:T(8,128)(2,1)}), bf16[4096,512]{1,0:T(8,128)(2,1)}) %all-gather.13.cloned.1.call-update) | async-done | bytes 4194320 | tf_op jit(solution)/shard_map/all_gather | solution.py:153
  235.7 8.7 %fusion.23 = f32[512,512]{1,0:T(8,128)S(1)} fusion(bf16[4096,512]{1,0:T(8,128)(2,1)} %all-gather.13.cloned.1.call-done, bf16[512,4096]{1,0:T(8,128)(2,1)} %bitcast.106, bf16[512,4096]{1,0:T(8,128)(2,1)} %bitcast.113, f32[4096]{0:T(1024)S(1)} %bitcast.124, bf16[5,32,4096]{2,1,0:T(8,128)(2,1)} %param.27, bf16[512,160]{0,1:T(8,128)(2,1)} %copy-done.23), kind=kOutput, calls=%fused_computation.48 | convolution fusion | flops 2296381440 | bytes 13942784 | tf_op jit(solution)/shard_map/dot_general | solution.py:159
  250.1 6.3 %exponential_multiply_fusion = (f32[32,16,8,64]{3,2,1,0:T(8,128)}, f32[32,16,8,64]{3,2,1,0:T(8,128)}, f32[32,16,8]{2,1,0:T(8,128)S(1)}, f32[32,16,8,64]{3,2,1,0:T(8,128)S(1)}) fusion(f32[32,16,8,64]{3,2,1,0:T(8,128)} %mul.162, f32[32,16,8,64]{3,2,1,0:T(8,128)S(1)} %fusion.79, f32[32,8,64]{2,1,0:T(8,128)S(1)} %get-tuple-element.4, ...), kind=kLoop, calls=%fused_computation.36 | loop fusion | flops 1830912 | bytes 6375936 | tf_op jit(solution)/shard_map/mul | solution.py:91
  256.4 13.1 %multiply_reduce_fusion = f32[32,16,16,8]{3,2,1,0:T(8,128)} fusion(f32[32,16,8,64]{3,2,1,0:T(8,128)S(1)} %fusion.79, f32[32,16,8,64]{3,2,1,0:T(8,128)S(1)} %get-tuple-element.10, f32[32,16,8,64]{3,2,1,0:T(8,128)S(1)} %copy-done.3, f32[32,16,8,64]{3,2,1,0:T(8,128)S(1)} %copy-done.2, pred[16,16]{1,0:T(8,128)(4,1)S(1)} %iota_compare_fusion.3), kind=kLoop, calls=%fused_computation.7 | loop fusion | flops 20905984 | bytes 4456704 | tf_op jit(solution)/shard_map/reduce_sum | solution.py:79
  273.4 43.0 %all-gather.11.cloned.1.call-done = bf16[4096,512]{1,0:T(8,128)(2,1)} async-done(((bf16[1024,512]{1,0:T(8,128)(2,1)}), bf16[4096,512]{1,0:T(8,128)(2,1)}) %all-gather.11.cloned.1.call-update) | async-done | bytes 4194320 | tf_op jit(solution)/shard_map/all_gather | solution.py:154
  316.4 8.6 %fusion.24 = f32[512,512]{1,0:T(8,128)S(1)} fusion(bf16[4096,512]{1,0:T(8,128)(2,1)} %all-gather.11.cloned.1.call-done, bf16[512,4096]{1,0:T(8,128)(2,1)} %bitcast.107, bf16[512,4096]{1,0:T(8,128)(2,1)} %bitcast.114, f32[4096]{0:T(1024)S(1)} %bitcast.123, bf16[5,32,4096]{2,1,0:T(8,128)(2,1)} %param.27, bf16[512,160]{0,1:T(8,128)(2,1)} %copy-done.23), kind=kOutput, calls=%fused_computation.49 | convolution fusion | flops 2296381440 | bytes 13942784 | tf_op jit(solution)/shard_map/dot_general | solution.py:159
  327.3 10.2 %fusion.12 = f32[32,8,16,64]{3,2,1,0:T(8,128)S(1)} fusion(f32[32,8,64,64]{3,2,1,0:T(8,128)} %param.23, f32[32,16,8,64]{3,2,1,0:T(8,128)S(1)} %copy-done.7), kind=kOutput, calls=%fused_computation.34 | convolution fusion | flops 201326592 | bytes 6291456 | tf_op jit(solution)/shard_map/bthi,bhij->bthj/dot_general | solution.py:70
  348.3 19.7 %multiply_add_fusion = bf16[32,8,64,64]{3,2,1,0:T(8,128)(2,1)} fusion(f32[32,8,64,64]{3,2,1,0:T(8,128)} %param.23, f32[32,8,64]{2,1,0:T(8,128)S(1)} %get-tuple-element.3, f32[32,16,8,64]{3,2,1,0:T(8,128)} %get-tuple-element.7, f32[32,16,8,64]{3,2,1,0:T(8,128)} %reshape.356), kind=kOutput, calls=%fused_computation.23 | convolution fusion | flops 204472320 | bytes 8454144 | tf_op jit(solution)/shard_map/bshi,bshj->bhij/dot_general | solution.py:92
  368.0 7.6 %gather_fusion = bf16[64,8,64,64]{3,2,1,0:T(8,128)(2,1)} fusion(bf16[32,8,64,64]{3,2,1,0:T(8,128)(2,1)} %multiply_add_fusion, s32[1024]{0:T(1024)S(1)} %pad_clamp_fusion.2), kind=kCustom, calls=%fused_computation | custom fusion | bytes 8388864 | tf_op jit(solution)/shard_map/gather | solution.py:228
  380.6 10.4 %select_convert_fusion = bf16[4,16,8,64,64]{4,3,2,1,0:T(8,128)(2,1)} fusion(bf16[4,16,8,64,64]{4,3,2,1,0:T(8,128)(2,1)} %bitcast.102, pred[4,16]{1,0:T(4,128)(4,1)S(1)} %and_reduce_fusion), kind=kLoop, calls=%fused_computation.15 | loop fusion | flops 2097152 | bytes 8388672 | tf_op jit(solution)/shard_map/convert_element_type | solution.py:235
  397.7 9.5 %reshape.439 = bf16[4,2,262144]{2,1,0:T(2,128)(2,1)} reshape(bf16[4,16,8,64,64]{4,3,2,1,0:T(8,128)(2,1)} %select_convert_fusion) | data formatting | bytes 8388608
  412.7 9.6 %multiply_convert_fusion = bf16[512,512]{1,0:T(8,128)(2,1)} fusion(bf16[4096,512]{1,0:T(8,128)(2,1)} %all-gather.15.cloned.1.call-done, bf16[512,4096]{1,0:T(8,128)(2,1)} %bitcast.108, bf16[512,4096]{1,0:T(8,128)(2,1)} %bitcast.115, f32[4096]{0:T(1024)S(1)} %bitcast.122, f32[512,512]{1,0:T(8,128)S(1)} %copy.79, f32[512,512]{1,0:T(8,128)S(1)} %reshape.357, ...), kind=kOutput, calls=%fused_computation.58 | convolution fusion | flops 2299002880 | bytes 16568320 | tf_op jit(solution)/shard_map/dot_general | solution.py:159
  422.3 6.6 %convolution_convert_fusion = bf16[512,4096]{1,0:T(8,128)(2,1)} fusion(bf16[512,512]{1,0:T(8,128)(2,1)} %multiply_convert_fusion, bf16[512,8192]{1,0:T(8,128)(2,1)} %constant_dynamic-update-slice_fusion, s32[]{:T(128)S(6)} %select_n.128), kind=kOutput, calls=%fused_computation.24 | convolution fusion | flops 2149580800 | bytes 8912900 | tf_op jit(solution)/shard_map/dot_general | solution.py:192
  431.9 73.8 %all-to-all-done = bf16[4,2,262144]{2,1,0:T(2,128)(2,1)} async-done(((bf16[4,2,262144]{2,1,0:T(2,128)(2,1)}), bf16[4,2,262144]{2,1,0:T(2,128)(2,1)}, u32[]{:S(2)}, u32[]{:S(2)}) %all-to-all-start) | async-done | bytes 4194336 | tf_op jit(solution)/shard_map/all_to_all | solution.py:234
  505.7 9.3 %reshape.440 = bf16[4,16,8,64,64]{4,3,2,1,0:T(8,128)(2,1)} reshape(bf16[4,2,262144]{2,1,0:T(2,128)(2,1)} %all-to-all-done) | data formatting | bytes 8388608
  515.0 11.3 %bitcast_convert_fusion = f32[64,8,64,64]{3,2,1,0:T(8,128)} fusion(bf16[4,16,8,64,64]{4,3,2,1,0:T(8,128)(2,1)} %reshape.440), kind=kLoop, calls=%fused_computation.22 | loop fusion | flops 2097152 | bytes 12582912 | tf_op jit(solution)/shard_map/reshape | solution.py:246
  526.3 10.4 %gather_fusion.2 = f32[32,8,64,64]{3,2,1,0:T(8,128)} fusion(f32[64,8,64,64]{3,2,1,0:T(8,128)} %bitcast_convert_fusion, s32[1024]{0:T(1024)S(1)} %pad_clamp_fusion), kind=kCustom, calls=%fused_computation.2 | custom fusion | bytes 8388736 | tf_op jit(solution)/shard_map/gather | solution.py:246
  (148 shorter events, 81.4 us)
Async XLA Ops:
  7.2 125.4 %copy-start = (bf16[4096,160]{0,1:T(8,128)(2,1)S(1)}, bf16[4096,160]{0,1:T(8,128)(2,1)}, u32[]{:S(2)}) copy-start(bf16[4096,160]{0,1:T(8,128)(2,1)} %param.26) | copy-start | bytes 3932164
  7.2 6.0 %copy-start.22 = (s32[128]{0:T(128)S(1)}, s32[128]{0:T(128)}, u32[]{:S(2)}) copy-start(s32[128]{0:T(128)} %param.41) | copy-start | bytes 1540
  7.2 31.3 %copy-start.16 = (s32[128]{0:T(128)S(1)}, s32[128]{0:T(128)}, u32[]{:S(2)}) copy-start(s32[128]{0:T(128)} %param.40) | copy-start | bytes 1540
  7.2 121.7 %all-gather.7.cloned.1.call-start = ((), (), s32[]{:S(2)}) async-start(), calls=%async_computation.3 | async-start | bytes 4718592 | tf_op jit(solution)/shard_map/all_gather | solution.py:138
  7.9 147.3 %all-gather.9.cloned.1.call-start = ((), (), s32[]{:S(2)}) async-start(), calls=%async_computation.4 | async-start | bytes 5242880 | tf_op jit(solution)/shard_map/all_gather | solution.py:152
  8.7 227.0 %all-gather.13.cloned.1.call-start = ((), (), s32[]{:S(2)}) async-start(), calls=%async_computation.6 | async-start | bytes 5242880 | tf_op jit(solution)/shard_map/all_gather | solution.py:153
  9.4 307.0 %all-gather.11.cloned.1.call-start = ((), (), s32[]{:S(2)}) async-start(), calls=%async_computation.5 | async-start | bytes 5242880 | tf_op jit(solution)/shard_map/all_gather | solution.py:154
  10.0 402.7 %all-gather.15.cloned.1.call-start = ((), (), s32[]{:S(2)}) async-start(), calls=%async_computation.7 | async-start | bytes 5242880 | tf_op jit(solution)/shard_map/all_gather | solution.py:155
  10.0 28.5 %collective-permute-start = (bf16[512,1024]{1,0:T(8,128)(2,1)}, bf16[512,1024]{1,0:T(8,128)(2,1)S(1)}, u32[]{:S(2)}, u32[]{:S(2)}) collective-permute-start(bf16[512,1024]{1,0:T(8,128)(2,1)} %param.36), channel_id=1, source_target_pairs={{0,8},{8,16},{16,24},{24,0},{1,9},{9,17},{17,25},{25,1},{2,10},{10... | collective-permute-start | bytes 3145736 | tf_op jit(solution)/shard_map/ppermute | solution.py:14
  13.3 107.9 %copy-start.9 = (bf16[512,1024]{1,0:T(8,128)(2,1)S(1)}, bf16[512,1024]{1,0:T(8,128)(2,1)}, u32[]{:S(2)}) copy-start(bf16[512,1024]{1,0:T(8,128)(2,1)} %param.36) | copy-start | bytes 3145732
  38.5 28.0 %collective-permute-start.1 = (bf16[512,1024]{1,0:T(8,128)(2,1)S(1)}, bf16[512,1024]{1,0:T(8,128)(2,1)}, u32[]{:S(2)}, u32[]{:S(2)}) collective-permute-start(bf16[512,1024]{1,0:T(8,128)(2,1)S(1)} %collective-permute-done), channel_id=1, source_target_pairs={{0,8},{8,16},{16,24},{24,0},{1,9},{9,17},{17,25},{25,1},{2,10},{10... | collective-permute-start | bytes 3145736 | tf_op jit(solution)/shard_map/ppermute | solution.py:14
  66.5 49.1 %collective-permute-start.2 = (bf16[512,1024]{1,0:T(8,128)(2,1)}, bf16[512,1024]{1,0:T(8,128)(2,1)}, u32[]{:S(2)}, u32[]{:S(2)}) collective-permute-start(bf16[512,1024]{1,0:T(8,128)(2,1)} %collective-permute-done.1), channel_id=1, source_target_pairs={{0,8},{8,16},{16,24},{24,0},{1,9},{9,17},{17,25},{25,1},{2,10},{10... | collective-permute-start | bytes 3145736 | tf_op jit(solution)/shard_map/ppermute | solution.py:14
  134.6 7.0 %copy-start.23 = (bf16[512,160]{0,1:T(8,128)(2,1)}, bf16[512,160]{0,1:T(8,128)(2,1)S(1)}, u32[]{:S(2)}) copy-start(bf16[512,160]{0,1:T(8,128)(2,1)S(1)} %fusion.29) | copy-start | bytes 491524
  134.6 7.0 %copy-start.13 = (bf16[64,512]{1,0:T(8,128)(2,1)S(1)}, bf16[64,512]{1,0:T(8,128)(2,1)}, u32[]{:S(2)}) copy-start(bf16[64,512]{1,0:T(8,128)(2,1)} %param.30) | copy-start | bytes 196612
  134.6 7.0 %copy-start.15 = (f32[512]{0:T(512)S(1)}, f32[512]{0:T(512)}, u32[]{:S(2)}) copy-start(f32[512]{0:T(512)} %param.28) | copy-start | bytes 6148
  250.1 6.3 %copy-start.2 = (f32[32,16,8,64]{3,2,1,0:T(8,128)S(1)}, f32[32,16,8,64]{3,2,1,0:T(8,128)}, u32[]{:S(2)}) copy-start(f32[32,16,8,64]{3,2,1,0:T(8,128)} %reshape.354) | copy-start | bytes 3145732
  250.1 6.3 %copy-start.3 = (f32[32,16,8,64]{3,2,1,0:T(8,128)S(1)}, f32[32,16,8,64]{3,2,1,0:T(8,128)}, u32[]{:S(2)}) copy-start(f32[32,16,8,64]{3,2,1,0:T(8,128)} %mul.162) | copy-start | bytes 3145732
  327.3 10.2 %copy-start.4 = (f32[32,16,8,64]{3,2,1,0:T(8,128)S(1)}, f32[32,16,8,64]{3,2,1,0:T(8,128)}, u32[]{:S(2)}) copy-start(f32[32,16,8,64]{3,2,1,0:T(8,128)} %reshape.356) | copy-start | bytes 3145732
  327.3 10.2 %copy-start.6 = (f32[32,16,16,8]{2,1,3,0:T(8,128)S(1)}, f32[32,16,16,8]{2,1,3,0:T(8,128)}, u32[]{:S(2)}) copy-start(f32[32,16,16,8]{2,1,3,0:T(8,128)} %copy.69) | copy-start | bytes 786436
  377.1 30.1 %all-to-all-start.1 = ((bf16[4,16,512]{2,1,0:T(8,128)(2,1)}), bf16[4,16,512]{2,1,0:T(8,128)(2,1)S(1)}, u32[]{:S(2)}, u32[]{:S(2)}) async-start(bf16[4,16,512]{2,1,0:T(8,128)(2,1)} %fusion.57), calls=%async_computation.2 | async-start | bytes 131072 | tf_op jit(solution)/shard_map/all_to_all | solution.py:237
  407.2 98.5 %all-to-all-start = ((bf16[4,2,262144]{2,1,0:T(2,128)(2,1)}), bf16[4,2,262144]{2,1,0:T(2,128)(2,1)}, u32[]{:S(2)}, u32[]{:S(2)}) async-start(bf16[4,2,262144]{2,1,0:T(2,128)(2,1)} %reshape.439), calls=%async_computation.1 | async-start | bytes 8388608 | tf_op jit(solution)/shard_map/all_to_all | solution.py:234
  412.4 124.3 %reduce-scatter.2.cloned.1.call-start = ((), (), s32[]{:S(2)}) async-start(), calls=%async_computation.8 | async-start | bytes 4718592 | tf_op jit(solution)/shard_map/reduce_scatter | solution.py:191
  526.3 10.4 %copy-start.11 = (bf16[4,16,4096]{2,1,0:T(8,128)(2,1)S(1)}, bf16[4,16,4096]{2,1,0:T(8,128)(2,1)}, u32[]{:S(2)}) copy-start(bf16[4,16,4096]{2,1,0:T(8,128)(2,1)} %param.21) | copy-start | bytes 1572868
  526.3 12.5 %copy-start.1 = (bf16[4096,160]{0,1:T(8,128)(2,1)S(1)}, bf16[4096,160]{0,1:T(8,128)(2,1)}, u32[]{:S(2)}) copy-start(bf16[4096,160]{0,1:T(8,128)(2,1)} %param.26) | copy-start | bytes 3932164
  (11 other events, 41.3 us)
Sparse Core Ops, SparseCore 0:
  9.9 39.4 all-gather.6
  50.9 104.2 all-gather.8
  156.8 78.7 all-gather.12
  237.1 79.2 all-gather.10
  317.8 80.6 all-gather.14
  429.1 52.6 reduce-scatter.1
